TPU v7x, 256 devices: a whole 4x4x8 slice. The times are simulated.
256 devices in a mesh: rows: 64 (over z, y, core), cols: 4 (over x).
Axes of the slice: x: 4, y: 4, z: 8, core: 2. Of those that a mesh axis runs over, the one named last changes fastest.
Arguments:
- hblocks: float32 [512, 24, 128, 128], P('rows'), may hold values from -0.0546875 to 0.0546875
- col_index: int32 [512, 24], P('rows'), may hold values from 0 to 511, as said below
- right_side: float32 [512, 64, 128], P('rows', 'cols'), may hold values from -12 to 12
- center: float32 [1], replicated, may hold values from -0.5 to 0.5
- shifts: float32 [8], replicated, may hold values from 0.05 to 2
- filter_weights: float32 [8], replicated, may hold values from 0.03 to 0.3
Outputs:
- filtered: float32 [512, 64, 128], P('rows', 'cols')
- gram_matrix: float32 [64, 64], P(None, 'cols')
- ritz_matrix: float32 [64, 64], P(None, 'cols')
Inputs may be any that keep to these rules, and one draw needn't show every extreme that they name: `col_index`: block rows are held 8 to a device of rows, in order. In block row i the first 8 column indices are the 8 block rows of the device that holds i, each once. Every other column index of a block row lies on another device of rows; for each pair of distinct devices, the block rows of the one that are named by the block rows of the other are exactly 2 distinct ones.
All inputs are finite; a program needn't handle non-finite values.
Results may differ from a plain program's by a relative error of at most 0.0001.
Values sent between devices are 32-bit elements; how exact they have to be, the bound alone decides.
No kernel may reach another device: no remote copies, remote signals or barrier semaphores. Data moves between devices by JAX's collectives and lax.ppermute only.
A program may use at most 64 MiB of HBM per device.

v0:
```python
import jax
import jax.numpy as jnp
from jax import lax
from jax.sharding import PartitionSpec as P

CAP = 2
ITERS = 2


exact_mode = lax.Precision.HIGHEST


def column_dot(first_arr, second_arr):
    return jnp.sum(first_arr * second_arr, axis=(0, 2))


def ordered_lists(need_mask, slot_width):
    ranks = jnp.cumsum(need_mask, axis=1)
    positions = lax.broadcasted_iota(jnp.int32, need_mask.shape, 1)
    columns_out = []
    for slot in range(slot_width):
        hit = (need_mask > 0) & (ranks == slot + 1)
        columns_out.append(jnp.sum(jnp.where(hit, positions, 0), axis=1))
    lists = jnp.stack(columns_out, axis=1)
    live = jnp.sum(need_mask, axis=1, keepdims=True) > 0
    return jnp.where(live, lists, -1)


def shards(hblocks, col_index, right_side, center, shifts, filter_weights):
    block_rows = hblocks.shape[0]
    block_width = hblocks.shape[2]
    local_vecs = right_side.shape[1]
    pole_count = shifts.shape[0]
    peer_count = lax.axis_size("rows")
    slot_width = CAP
    device_index = lax.axis_index("rows")
    own_cols = col_index[:, :block_rows] - device_index * block_rows
    far_cols = col_index[:, block_rows:].reshape(-1)
    near_blocks = hblocks[:, :block_rows]
    far_blocks = hblocks[:, block_rows:]
    every_key = jnp.arange(peer_count * block_rows, dtype=jnp.int32)
    need_mask = (
        jnp.any(far_cols[:, None] == every_key[None, :], axis=0)
        .astype(jnp.int32)
        .reshape(peer_count, block_rows)
    )
    incoming_mask = lax.all_to_all(need_mask, "rows", split_axis=0, concat_axis=0, tiled=True)
    send_lists = ordered_lists(incoming_mask, slot_width)
    my_lists = ordered_lists(need_mask, slot_width)
    owners = lax.broadcasted_iota(jnp.int32, my_lists.shape, 0)
    slot_keys = jnp.where(my_lists >= 0, owners * block_rows + my_lists, -1).reshape(-1)
    slot_total = slot_keys.shape[0]
    matches = far_cols[:, None] == slot_keys[None, :]
    picker = matches.astype(jnp.float32)
    row_numbers = jnp.arange(block_rows, dtype=jnp.int32)[:, None]
    spread = (send_lists.reshape(-1)[None, :] == row_numbers).astype(jnp.float32)
    own_spread = (own_cols.reshape(-1)[None, :] == row_numbers).astype(jnp.float32)

    def apply_h(vector):
        whole_vec = lax.all_gather(vector, "rows", axis=0, tiled=True)
        far_vec = whole_vec[far_cols]
        far_vec = far_vec.reshape(block_rows, -1, local_vecs, block_width)
        near_vec = vector[own_cols]
        result = jnp.einsum("ikab,ikvb->iva", near_blocks, near_vec, precision=exact_mode)
        result = result + jnp.einsum("ikab,ikvb->iva", far_blocks, far_vec, precision=exact_mode)
        near_terms = jnp.einsum(
            "ikab,iva->ikvb", near_blocks, vector, precision=exact_mode
        ).reshape(block_rows * block_rows, -1)
        result = result + jnp.dot(own_spread, near_terms, precision=exact_mode).reshape(
            vector.shape
        )
        far_terms = jnp.einsum("ikab,iva->ikvb", far_blocks, vector, precision=exact_mode).reshape(
            far_cols.shape[0], -1
        )
        slot_sums = jnp.dot(picker.T, far_terms, precision=exact_mode).reshape(
            peer_count, slot_width, local_vecs, block_width
        )
        returned = lax.all_to_all(
            slot_sums, "rows", split_axis=0, concat_axis=0, tiled=True
        ).reshape(slot_total, -1)
        return result + jnp.dot(spread, returned, precision=exact_mode).reshape(vector.shape)

    center_value = center[0]
    base_shift = jnp.min(shifts)
    delta_shift = (shifts - base_shift)[:, None]
    residual = right_side
    solutions = jnp.zeros((pole_count,) + right_side.shape, jnp.float32)
    shifted_dirs = jnp.broadcast_to(right_side, solutions.shape)
    zeta_prev = jnp.ones((pole_count, local_vecs), jnp.float32)
    zeta_now = jnp.ones((pole_count, local_vecs), jnp.float32)
    alpha_prev = jnp.ones((local_vecs,), jnp.float32)
    beta_prev = jnp.zeros((local_vecs,), jnp.float32)

    def squares(vector):
        return lax.psum(column_dot(vector, vector), "rows")

    direction = right_side
    res_norm = squares(residual)
    for iteration in range(ITERS):
        shifted = apply_h(direction) - center_value * direction
        op_image = apply_h(shifted) - center_value * shifted + base_shift * direction
        alpha_now = res_norm / lax.psum(column_dot(direction, op_image), "rows")
        solution_solutions = solutions
        zeta_next = (
            zeta_now
            * zeta_prev
            * alpha_prev
            / (
                alpha_now * beta_prev * (zeta_prev - zeta_now)
                + zeta_prev * alpha_prev * (1.0 + delta_shift * alpha_now)
            )
        )
        zeta_ratio = zeta_next / zeta_now
        solution_solutions = (
            solution_solutions + (alpha_now * zeta_ratio)[:, None, :, None] * shifted_dirs
        )
        solutions, zeta_next, zeta_ratio = (solution_solutions, zeta_next, zeta_ratio)
        residual = residual - alpha_now[None, :, None] * op_image
        if iteration + 1 < ITERS:
            norm_next = squares(residual)
            beta_now = norm_next / res_norm
            direction = residual + beta_now[None, :, None] * direction
            shifted_dirs = (
                zeta_next[:, None, :, None] * residual[None]
                + (beta_now * zeta_ratio * zeta_ratio)[:, None, :, None] * shifted_dirs
            )
            zeta_prev, zeta_now, alpha_prev, beta_prev, res_norm = (
                zeta_now,
                zeta_next,
                alpha_now,
                beta_now,
                norm_next,
            )
    filtered = jnp.sum(filter_weights[:, None, None, None] * solutions, axis=0)
    applied = apply_h(filtered)
    column_piece = lax.all_gather(filtered, "cols", axis=1, tiled=True)
    correlation = jnp.einsum("iae,ibe->ab", column_piece, filtered, precision=exact_mode)
    projected = jnp.einsum("iae,ibe->ab", column_piece, applied, precision=exact_mode)
    partial_gram = jnp.stack([correlation, projected])
    summed = lax.psum(partial_gram, "rows")
    row_total = peer_count * block_rows * block_width
    return (filtered, summed[0] / row_total, summed[1] / row_total)


def solution(mesh):
    placed = (P("rows", None, None, None), P("rows", None), P("rows", "cols", None), P(), P(), P())
    return jax.shard_map(
        shards,
        mesh=mesh,
        in_specs=placed,
        out_specs=(P("rows", "cols", None), P(None, "cols"), P(None, "cols")),
        check_vma=False,
    )
```

profile of v0, /device:TPU:2, one launch (start us, length us, event | category | flops | bytes accessed | tf_op | source)
XLA Modules:
  0.0 1110.9 jit_solution(14288987445474949240)
XLA Ops:
  9.6 12.1 %all-to-all-start = ((s32[64,1,8]{2,1,0:T(1,128)}), s32[64,1,8]{2,1,0:T(1,128)S(1)}, u32[]{:S(2)}, u32[]{:S(2)}) async-start(s32[64,1,8]{2,1,0:T(1,128)} %bitcast.12), calls=%async_computation | async-start | bytes 65536 | tf_op jit(solution)/shard_map/all_to_all | solution.py:47
  22.1 6.4 fusion.16
  30.8 1.6 copy.118
  32.4 10.3 all-to-all-start.1
  43.8 3.8 fusion.40
  48.1 5.3 fusion.55
  55.2 17.0 %all-to-all-done.1 = f32[64,2,16,128]{3,2,1,0:T(8,128)S(1)} async-done(((f32[64,2,16,128]{3,2,1,0:T(8,128)}), f32[64,2,16,128]{3,2,1,0:T(8,128)S(1)}, u32[]{:S(2)}, u32[]{:S(2)}) %all-to-all-start.1) | async-done | bytes 1048608 | tf_op jit(solution)/shard_map/all_to_all | solution.py:78
  73.5 21.0 %all-gather.6.cloned.1.call-done = f32[512,16,128]{2,1,0:T(8,128)} async-done(((f32[8,16,128]{2,1,0:T(8,128)}), f32[512,16,128]{2,1,0:T(8,128)}) %all-gather.6.cloned.1.call-update) | async-done | bytes 4194320 | tf_op jit(solution)/shard_map/all_gather | solution.py:60
  94.5 2.8 gather_fusion.1
  97.3 10.0 fusion.148
  107.3 6.9 fusion.12
  117.2 6.8 all-to-all-start.2
  125.3 3.8 fusion.43
  129.5 5.3 fusion.58
  134.8 19.4 %all-to-all-done.2 = f32[64,2,16,128]{3,2,1,0:T(8,128)S(1)} async-done(((f32[64,2,16,128]{3,2,1,0:T(8,128)}), f32[64,2,16,128]{3,2,1,0:T(8,128)S(1)}, u32[]{:S(2)}, u32[]{:S(2)}) %all-to-all-start.2) | async-done | bytes 1048608 | tf_op jit(solution)/shard_map/all_to_all | solution.py:78
  155.5 31.8 %all-gather.8.cloned.1.call-done = f32[512,16,128]{2,1,0:T(8,128)} async-done(((f32[8,16,128]{2,1,0:T(8,128)}), f32[512,16,128]{2,1,0:T(8,128)}) %all-gather.8.cloned.1.call-update) | async-done | bytes 4194320 | tf_op jit(solution)/shard_map/all_gather | solution.py:60
  187.3 2.8 gather_fusion.3
  190.1 10.1 multiply_reduce_fusion.2
  200.3 126.4 %all-reduce = (f32[16]{0:T(128)S(1)}, f32[16]{0:T(128)S(1)}) all-reduce(f32[16]{0:T(128)S(1)} %get-tuple-element.4, f32[16]{0:T(128)S(1)} %get-tuple-element.3), channel_id=1, replica_groups=mesh['rows'=64,'cols'=4] {'rows'}, use_global_device_ids=true, to_apply=%region_1.0 | all-reduce | flops 32 | bytes 256 | tf_op jit(solution)/shard_map/psum | solution.py:95
  326.9 124.1 %psum.37 = f32[16]{0:T(128)S(1)} all-reduce(f32[16]{0:T(128)S(1)} %get-tuple-element.15), channel_id=1, replica_groups=mesh['rows'=64,'cols'=4] {'rows'}, use_global_device_ids=true, to_apply=%region_15.16 | all-reduce | flops 16 | bytes 128 | tf_op jit(solution)/shard_map/psum | solution.py:95
  451.7 6.4 fusion.8
  459.5 1.6 copy.130
  461.1 6.2 all-to-all-start.3
  468.0 4.0 fusion.46
  472.4 5.3 fusion.61
  477.7 20.2 %all-to-all-done.3 = f32[64,2,16,128]{3,2,1,0:T(8,128)S(1)} async-done(((f32[64,2,16,128]{3,2,1,0:T(8,128)}), f32[64,2,16,128]{3,2,1,0:T(8,128)S(1)}, u32[]{:S(2)}, u32[]{:S(2)}) %all-to-all-start.3) | async-done | bytes 1048608 | tf_op jit(solution)/shard_map/all_to_all | solution.py:78
  499.1 31.0 %all-gather.10.cloned.1.call-done = f32[512,16,128]{2,1,0:T(8,128)} async-done(((f32[8,16,128]{2,1,0:T(8,128)}), f32[512,16,128]{2,1,0:T(8,128)}) %all-gather.10.cloned.1.call-update) | async-done | bytes 4194320 | tf_op jit(solution)/shard_map/all_gather | solution.py:60
  530.1 2.8 gather_fusion.5
  533.0 10.0 fusion.121
  543.0 6.4 fusion.4
  552.4 6.7 all-to-all-start.4
  559.8 3.8 fusion.49
  564.0 5.3 fusion.64
  569.3 20.1 %all-to-all-done.4 = f32[64,2,16,128]{3,2,1,0:T(8,128)S(1)} async-done(((f32[64,2,16,128]{3,2,1,0:T(8,128)}), f32[64,2,16,128]{3,2,1,0:T(8,128)S(1)}, u32[]{:S(2)}, u32[]{:S(2)}) %all-to-all-start.4) | async-done | bytes 1048608 | tf_op jit(solution)/shard_map/all_to_all | solution.py:78
  590.7 31.8 %all-gather.12.cloned.1.call-done = f32[512,16,128]{2,1,0:T(8,128)} async-done(((f32[8,16,128]{2,1,0:T(8,128)}), f32[512,16,128]{2,1,0:T(8,128)}) %all-gather.12.cloned.1.call-update) | async-done | bytes 4194320 | tf_op jit(solution)/shard_map/all_gather | solution.py:60
  622.5 2.8 gather_fusion.7
  625.3 10.1 fusion.151
  636.1 126.4 %psum.38 = f32[16]{0:T(128)S(1)} all-reduce(f32[16]{0:T(128)S(1)} %fusion.151), channel_id=1, replica_groups=mesh['rows'=64,'cols'=4] {'rows'}, use_global_device_ids=true, to_apply=%region_17.18 | all-reduce | flops 16 | bytes 128 | tf_op jit(solution)/shard_map/psum | solution.py:102
  763.5 6.4 fusion
  772.9 6.4 all-to-all-start.5
  780.0 12.3 %all_gather.22 = f32[8,64,128]{2,1,0:T(8,128)S(1)} all-gather(f32[8,16,128]{2,1,0:T(8,128)S(1)} %copy-done.1), channel_id=1, replica_groups=mesh['rows'=64,'cols'=4] {'cols'}, dimensions={1}, use_global_device_ids=true | all-gather | bytes 327680 | tf_op jit(solution)/shard_map/all_gather | solution.py:136
  792.5 3.9 fusion.52
  796.8 5.3 fusion.67
  802.1 7.5 all-to-all-done.5
  810.9 31.5 %all-gather.14.cloned.1.call-done = f32[512,16,128]{2,1,0:T(8,128)} async-done(((f32[8,16,128]{2,1,0:T(8,128)}), f32[512,16,128]{2,1,0:T(8,128)}) %all-gather.14.cloned.1.call-update) | async-done | bytes 4194320 | tf_op jit(solution)/shard_map/all_gather | solution.py:60
  842.4 2.8 gather_fusion.9
  845.2 9.3 fusion.91
  854.9 248.5 %psum.39 = f32[2,64,16]{1,2,0:T(8,128)S(1)} all-reduce(f32[2,64,16]{1,2,0:T(8,128)S(1)} %pad_maximum_fusion), channel_id=1, replica_groups=mesh['rows'=64,'cols'=4] {'rows'}, use_global_device_ids=true, to_apply=%region_19.20 | all-reduce | flops 2048 | bytes 16384 | tf_op jit(solution)/shard_map/psum | solution.py:140
  (109 shorter events, 32.8 us)
Async XLA Ops:
  7.2 87.3 %all-gather.6.cloned.1.call-start = ((), (), s32[]{:S(2)}) async-start(), calls=%async_computation.6 | async-start | bytes 4259840 | tf_op jit(solution)/shard_map/all_gather | solution.py:60
  9.6 22.8 %all-to-all-start = ((s32[64,1,8]{2,1,0:T(1,128)}), s32[64,1,8]{2,1,0:T(1,128)S(1)}, u32[]{:S(2)}, u32[]{:S(2)}) async-start(s32[64,1,8]{2,1,0:T(1,128)} %bitcast.12), calls=%async_computation | async-start | bytes 65536 | tf_op jit(solution)/shard_map/all_to_all | solution.py:47
  22.1 20.9 %copy-start.5 = (s32[8,24]{1,0:T(8,128)S(1)}, s32[8,24]{1,0:T(8,128)}, u32[]{:S(2)}) copy-start(s32[8,24]{1,0:T(8,128)} %param.7) | copy-start | bytes 2308
  22.1 21.1 %copy-start = (f32[8,16,128]{2,1,0:T(8,128)S(1)}, f32[8,16,128]{2,1,0:T(8,128)}, u32[]{:S(2)}) copy-start(f32[8,16,128]{2,1,0:T(8,128)} %param.8) | copy-start | bytes 196612
  32.4 39.8 %all-to-all-start.1 = ((f32[64,2,16,128]{3,2,1,0:T(8,128)}), f32[64,2,16,128]{3,2,1,0:T(8,128)S(1)}, u32[]{:S(2)}, u32[]{:S(2)}) async-start(f32[64,2,16,128]{3,2,1,0:T(8,128)} %copy.118), calls=%async_computation.1 | async-start | bytes 2097152 | tf_op jit(solution)/shard_map/all_to_all | solution.py:78
  42.7 144.6 %all-gather.8.cloned.1.call-start = ((), (), s32[]{:S(2)}) async-start(), calls=%async_computation.7 | async-start | bytes 4259840 | tf_op jit(solution)/shard_map/all_gather | solution.py:60
  107.3 16.7 %copy-start.7 = (f32[8]{0:T(128)S(1)}, f32[8]{0:T(128)}, u32[]{:S(2)}) copy-start(f32[8]{0:T(128)} %param.10) | copy-start | bytes 100
  107.3 17.3 %copy-start.3 = (f32[8,16,128]{2,1,0:T(8,128)S(1)}, f32[8,16,128]{2,1,0:T(8,128)}, u32[]{:S(2)}) copy-start(f32[8,16,128]{2,1,0:T(8,128)} %fusion.148) | copy-start | bytes 196612
  117.2 37.0 %all-to-all-start.2 = ((f32[64,2,16,128]{3,2,1,0:T(8,128)}), f32[64,2,16,128]{3,2,1,0:T(8,128)S(1)}, u32[]{:S(2)}, u32[]{:S(2)}) async-start(f32[64,2,16,128]{3,2,1,0:T(8,128)} %copy.124), calls=%async_computation.2 | async-start | bytes 2097152 | tf_op jit(solution)/shard_map/all_to_all | solution.py:78
  124.0 406.2 %all-gather.10.cloned.1.call-start = ((), (), s32[]{:S(2)}) async-start(), calls=%async_computation.8 | async-start | bytes 4259840 | tf_op jit(solution)/shard_map/all_gather | solution.py:60
  451.6 15.7 %copy-start.2 = (f32[8,16,128]{2,1,0:T(8,128)S(1)}, f32[8,16,128]{2,1,0:T(8,128)}, u32[]{:S(2)}) copy-start(f32[8,16,128]{2,1,0:T(8,128)} %multiply_add_fusion) | copy-start | bytes 196612
  461.1 36.8 %all-to-all-start.3 = ((f32[64,2,16,128]{3,2,1,0:T(8,128)}), f32[64,2,16,128]{3,2,1,0:T(8,128)S(1)}, u32[]{:S(2)}, u32[]{:S(2)}) async-start(f32[64,2,16,128]{3,2,1,0:T(8,128)} %copy.130), calls=%async_computation.3 | async-start | bytes 2097152 | tf_op jit(solution)/shard_map/all_to_all | solution.py:78
  467.3 155.2 %all-gather.12.cloned.1.call-start = ((), (), s32[]{:S(2)}) async-start(), calls=%async_computation.9 | async-start | bytes 4259840 | tf_op jit(solution)/shard_map/all_gather | solution.py:60
  543.0 16.1 %copy-start.4 = (f32[8,16,128]{2,1,0:T(8,128)S(1)}, f32[8,16,128]{2,1,0:T(8,128)}, u32[]{:S(2)}) copy-start(f32[8,16,128]{2,1,0:T(8,128)} %fusion.121) | copy-start | bytes 196612
  552.4 37.0 %all-to-all-start.4 = ((f32[64,2,16,128]{3,2,1,0:T(8,128)}), f32[64,2,16,128]{3,2,1,0:T(8,128)S(1)}, u32[]{:S(2)}, u32[]{:S(2)}) async-start(f32[64,2,16,128]{3,2,1,0:T(8,128)} %copy.136), calls=%async_computation.4 | async-start | bytes 2097152 | tf_op jit(solution)/shard_map/all_to_all | solution.py:78
  559.1 283.3 %all-gather.14.cloned.1.call-start = ((), (), s32[]{:S(2)}) async-start(), calls=%async_computation.10 | async-start | bytes 4259840 | tf_op jit(solution)/shard_map/all_gather | solution.py:60
  589.4 173.1 %copy-start.6 = (f32[8]{0:T(128)S(1)}, f32[8]{0:T(128)}, u32[]{:S(2)}) copy-start(f32[8]{0:T(128)} %param.11) | copy-start | bytes 100
  763.5 15.9 %copy-start.1 = (f32[8,16,128]{2,1,0:T(8,128)S(1)}, f32[8,16,128]{2,1,0:T(8,128)}, u32[]{:S(2)}) copy-start(f32[8,16,128]{2,1,0:T(8,128)} %multiply_reduce_fusion) | copy-start | bytes 196612
  772.9 36.7 %all-to-all-start.5 = ((f32[64,2,16,128]{3,2,1,0:T(8,128)}), f32[64,2,16,128]{3,2,1,0:T(8,128)S(1)}, u32[]{:S(2)}, u32[]{:S(2)}) async-start(f32[64,2,16,128]{3,2,1,0:T(8,128)} %copy.142), calls=%async_computation.5 | async-start | bytes 2097152 | tf_op jit(solution)/shard_map/all_to_all | solution.py:78
Sparse Core Ops, SparseCore 0:
  10.8 83.6 all-gather.5
  107.4 79.8 all-gather.7
  451.8 78.3 all-gather.9
  543.1 79.3 all-gather.11
  763.6 78.7 all-gather.13
where the time goes:
time: 1120 us; the launch traced here: 1110 us
  blocking collectives  638 us (57%)
  waiting for transfers between devices  232 us (21%)
  matrix products  137 us (12%)
  starting transfers between devices  48.9 us (4%)
  local copies, waits for them, and re-layouts  34 us (3%)
  between operations  15.5 us (1%)
    psum x2, blocking collectives, squares(): return lax.psum(column_dot(vector, vector), 'rows')  250 us
    psum x1, blocking collectives, shards(): summed = lax.psum(partial_gram, 'rows')  248 us
    all_gather x5, waiting for transfers between devices, apply_h(): whole_vec = lax.all_gather(vector, 'rows', axis=0, tiled=True)  147 us
    psum x1, blocking collectives, shards(): alpha_now = res_norm / lax.psum(column_dot(direction, op_image), 'rows')  126 us
    all_to_all x5, waiting for transfers between devices, apply_h(): lax.all_to_all(slot_sums, 'rows', split_axis=0, concat_axis=0, tiled=True)  84.2 us
    dot_general x5, matrix products, apply_h(): jnp.einsum('ikab,ikvb->iva', far_blocks, far_vec, precision=exact_mode)  49.5 us
    all_to_all x5, starting transfers between devices, apply_h(): lax.all_to_all(slot_sums, 'rows', split_axis=0, concat_axis=0, tiled=True)  36.3 us
    dot_general x5, matrix products, apply_h(): jnp.einsum('ikab,iva->ikvb', far_blocks, vector, precision=exact_mode)  32.6 us
  transfers between devices with their start and end apart: 11, of which 10 were waited for; matrix products, arithmetic and copies ran while one was open for 10% of the time, Pallas kernels for 0%

commit v1 on v0

v1 whole, which is shorter than its diff:
```python
import functools

import jax
import jax.numpy as jnp
from jax import lax
from jax.experimental import pallas as pl
from jax.experimental.pallas import tpu as pltpu
from jax.sharding import PartitionSpec as P

F32 = jnp.float32
BF16 = jnp.bfloat16
ROWS = 8
NEAR = 8
FAR = 16
VEC = 16
BLK = 128
PLANE = 8
DEPTH = 8
SLOTS = 16
TOTAL_ROWS = 65536.0

PLANE_GROUPS = [[z * PLANE + p for p in range(PLANE)] for z in range(DEPTH)]
DEPTH_GROUPS = [[z * PLANE + p for z in range(DEPTH)] for p in range(PLANE)]

PARAMS = pltpu.CompilerParams(vmem_limit_bytes=48 * 1024 * 1024)


def two_parts(x):
    high = x.astype(BF16)
    return high, (x - high.astype(F32)).astype(BF16)


def fold(d):
    return (d[:VEC, :BLK] + d[VEC:, BLK:]) + d[VEC:, :BLK] + d[:VEC, BLK:]


def times_block(vs, parts):
    return fold(jnp.dot(vs, jnp.concatenate(parts, axis=1), preferred_element_type=F32))


def times_block_t(vs, parts):
    return fold(
        lax.dot_general(
            vs,
            jnp.concatenate(parts, axis=0),
            (((1,), (1,)), ((), ())),
            preferred_element_type=F32,
        )
    )


def local_kernel(units, idx_ref, v_ref, h_ref, *refs):
    extras, send_ref, w_ref = refs[:-2], refs[-2], refs[-1]
    i = pl.program_id(0)

    @pl.when(i == 0)
    def _():
        w_ref[...] = jnp.zeros_like(w_ref)
        send_ref[...] = jnp.zeros_like(send_ref)
        for p in range(PLANE):
            send_ref[p * units + SLOTS] = extras[0][...]
            if len(extras) > 1:
                send_ref[p * units + SLOTS + 1] = extras[1][p]

    vs = jnp.concatenate(two_parts(v_ref[i]), axis=0)
    forward = jnp.zeros((VEC, BLK), F32)
    for k in range(NEAR + FAR):
        parts = two_parts(h_ref[0, k])
        t = times_block(vs, parts)
        where = idx_ref[i, k]
        if k < NEAR:
            w_ref[where] += t
            ns = jnp.concatenate(two_parts(v_ref[where]), axis=0)
            forward = forward + times_block_t(ns, parts)
        else:
            send_ref[where + (where >> 4) * (units - SLOTS)] += t
    w_ref[i] += forward


def middle_kernel(units, list_ref, recv_ref, zall_ref, zacc_ref, send_ref):
    zacc_ref[...] = jnp.zeros_like(zacc_ref)
    part = recv_ref[SLOTS]
    for p in range(1, PLANE):
        part = part + recv_ref[p * units + SLOTS]
    zacc_ref[DEPTH * ROWS] = part
    for p in range(PLANE):
        for s in range(SLOTS):
            row = (s // 2) * ROWS + list_ref[p, s]
            zacc_ref[row] += recv_ref[p * units + s]
            send_ref[p * SLOTS + s] = zall_ref[row]


def far_kernel(stage, idx_ref, z_ref, scal_ref, v_ref, w_ref, far_ref, zsum_ref, tot_ref, ha_ref, hb_ref, *refs):
    i = pl.program_id(0)
    center, base = scal_ref[0], scal_ref[1]
    acc = w_ref[i] + zsum_ref[i] - center * v_ref[i]
    for k in range(FAR):
        h = ha_ref[0, k] if k < FAR // 2 else hb_ref[0, k - FAR // 2]
        ns = jnp.concatenate(two_parts(far_ref[idx_ref[i, NEAR + k]]), axis=0)
        acc = acc + times_block_t(ns, two_parts(h))
    if stage == 1:
        zbuf_ref, out_ref, part_ref = refs
        square = acc * acc
    elif stage == 2:
        b_ref, rr_ref, zbuf_ref, out_ref, part_ref = refs
        rr = rr_ref[0]
        alpha = rr / (tot_ref[0] + base * rr)
        acc = b_ref[i] - alpha * (acc + base * b_ref[i])
        square = acc * acc
    else:
        b_ref, g_ref, rr_ref, out_ref, part_ref = refs
        beta = tot_ref[0] / rr_ref[0]
        direction = v_ref[i] + beta * b_ref[i]
        moved = acc + beta * g_ref[i]
        square = moved * moved + base * (direction * direction)
    out_ref[i] = acc
    if stage < 3:
        @pl.when(i == 0)
        def _():
            zbuf_ref[...] = jnp.zeros_like(zbuf_ref)
        zbuf_ref[z_ref[0] * ROWS + i] = acc

    @pl.when(i == 0)
    def _():
        part_ref[...] = square

    @pl.when(i > 0)
    def _():
        part_ref[...] += square

    @pl.when(i == ROWS - 1)
    def _():
        part_ref[...] = jnp.broadcast_to(jnp.sum(part_ref[...], axis=1, keepdims=True), (VEC, BLK))


def whole(shape):
    return pl.BlockSpec(shape, lambda *_: (0,) * len(shape))


def local_products(units, idx, v, h, extras):
    return pl.pallas_call(
        functools.partial(local_kernel, units),
        grid_spec=pltpu.PrefetchScalarGridSpec(
            num_scalar_prefetch=1,
            grid=(ROWS,),
            in_specs=[
                whole((ROWS, VEC, BLK)),
                pl.BlockSpec((1, NEAR + FAR, BLK, BLK), lambda i, *_: (i, 0, 0, 0)),
            ]
            + [whole(e.shape) for e in extras],
            out_specs=[whole((PLANE * units, VEC, BLK)), whole((ROWS, VEC, BLK))],
        ),
        out_shape=[
            jax.ShapeDtypeStruct((PLANE * units, VEC, BLK), F32),
            jax.ShapeDtypeStruct((ROWS, VEC, BLK), F32),
        ],
        compiler_params=PARAMS,
        name="local_products",
    )(idx, v, h, *extras)


def middle(units, lists, recv, zall):
    return pl.pallas_call(
        functools.partial(middle_kernel, units),
        grid_spec=pltpu.PrefetchScalarGridSpec(
            num_scalar_prefetch=1,
            grid=(1,),
            in_specs=[whole((PLANE * units, VEC, BLK)), whole((DEPTH * ROWS, VEC, BLK))],
            out_specs=[
                whole((DEPTH * ROWS + 1, VEC, BLK)),
                whole((PLANE * SLOTS, VEC, BLK)),
            ],
        ),
        out_shape=[
            jax.ShapeDtypeStruct((DEPTH * ROWS + 1, VEC, BLK), F32),
            jax.ShapeDtypeStruct((PLANE * SLOTS, VEC, BLK), F32),
        ],
        compiler_params=PARAMS,
        name="middle",
    )(lists, recv, zall)


def far_products(stage, idx, my_z, scalars, v, w, far, zsum, h, *more):
    unit = pl.BlockSpec((1, VEC, BLK), lambda *_: (DEPTH * ROWS, 0, 0))
    vec = whole((ROWS, VEC, BLK))
    half = FAR // 2
    extra_specs = {1: [], 2: [vec, unit], 3: [vec, vec, unit]}[stage]
    out_specs = [vec, whole((VEC, BLK))]
    out_shape = [
        jax.ShapeDtypeStruct((ROWS, VEC, BLK), F32),
        jax.ShapeDtypeStruct((VEC, BLK), F32),
    ]
    if stage < 3:
        out_specs = [whole((DEPTH * ROWS, VEC, BLK))] + out_specs
        out_shape = [jax.ShapeDtypeStruct((DEPTH * ROWS, VEC, BLK), F32)] + out_shape
    return pl.pallas_call(
        functools.partial(far_kernel, stage),
        grid_spec=pltpu.PrefetchScalarGridSpec(
            num_scalar_prefetch=3,
            grid=(ROWS,),
            in_specs=[
                vec,
                vec,
                whole((PLANE * SLOTS, VEC, BLK)),
                pl.BlockSpec((ROWS, VEC, BLK), lambda i, idx, z, s: (z[0], 0, 0)),
                unit,
                pl.BlockSpec((1, half, BLK, BLK), lambda i, *_: (i, 1, 0, 0)),
                pl.BlockSpec((1, half, BLK, BLK), lambda i, *_: (i, 2, 0, 0)),
            ]
            + extra_specs,
            out_specs=out_specs,
        ),
        out_shape=out_shape,
        compiler_params=PARAMS,
        name="far_products",
    )(idx, my_z, scalars, v, w, far, zsum, zsum, h, h, *more)


def gram_kernel(all_ref, b_ref, r_ref, g_ref, gr_ref, out_ref):
    total = jnp.zeros((2 * 4 * VEC, 4 * VEC), F32)
    for i in range(ROWS):
        left = jnp.concatenate([all_ref[0, i], all_ref[1, i]], axis=0)
        right = jnp.concatenate([b_ref[i], r_ref[i], g_ref[i], gr_ref[i]], axis=0)
        total = total + lax.dot_general(
            left,
            right,
            (((1,), (1,)), ((), ())),
            precision=lax.Precision.HIGHEST,
            preferred_element_type=F32,
        )
    out_ref[...] = total


def shards(hblocks, col_index, right_side, center, shifts, filter_weights):
    device = lax.axis_index("rows").astype(jnp.int32)
    my_z = (device // PLANE).reshape(1)
    own_cols = col_index[:, :NEAR] - device * ROWS
    far_cols = col_index[:, NEAR:]
    flat = far_cols.reshape(-1)
    owner = flat // ROWS
    smaller = (owner[:, None] == owner[None, :]) & (flat[None, :] < flat[:, None])
    slot = jnp.any(smaller, axis=1).astype(jnp.int32)
    flat_slot = (owner % PLANE) * SLOTS + (owner // PLANE) * 2 + slot
    idx = jnp.concatenate([own_cols, flat_slot.reshape(ROWS, FAR)], axis=1)
    named = flat_slot[None, :] == jnp.arange(PLANE * SLOTS, dtype=jnp.int32)[:, None]
    lists = jnp.max(jnp.where(named, (flat % ROWS)[None, :], 0), axis=1)
    lists_out = jnp.pad(
        lists.astype(F32).reshape(PLANE, 1, SLOTS), ((0, 0), (0, VEC - 1), (0, BLK - SLOTS))
    )

    base_shift = jnp.min(shifts)
    scalars = jnp.stack([center[0], base_shift])
    b = right_side
    part = jnp.broadcast_to(jnp.sum(b * b, axis=(0, 2))[:, None], (VEC, BLK))
    zbuf = lax.dynamic_update_slice(
        jnp.zeros((DEPTH * ROWS, VEC, BLK), F32), b, (my_z[0] * ROWS, 0, 0)
    )

    def plane_exchange(x):
        return lax.all_to_all(
            x, "rows", split_axis=0, concat_axis=0, tiled=True, axis_index_groups=PLANE_GROUPS
        )

    def depth_sum(x):
        return lax.psum(x, "rows", axis_index_groups=DEPTH_GROUPS)

    units = SLOTS + 2
    send, w = local_products(units, idx, b, hblocks, [part, lists_out])
    recv = plane_exchange(send)
    zall = depth_sum(zbuf)
    peer_lists = recv.reshape(PLANE, units, VEC, BLK)[:, SLOTS + 1, 0, :SLOTS].astype(jnp.int32)
    zacc, send = middle(units, peer_lists, recv, zall)
    far = plane_exchange(send)
    zsum1 = depth_sum(zacc)
    zbuf, g0, part = far_products(1, idx, my_z, scalars, b, w, far, zsum1, hblocks)

    units = SLOTS + 1
    send, w = local_products(units, idx, g0, hblocks, [part])
    recv = plane_exchange(send)
    zall = depth_sum(zbuf)
    zacc, send = middle(units, peer_lists, recv, zall)
    far = plane_exchange(send)
    zsum2 = depth_sum(zacc)
    zbuf, r1, part = far_products(2, idx, my_z, scalars, g0, w, far, zsum2, hblocks, b, zsum1)

    send, w = local_products(units, idx, r1, hblocks, [part])
    recv = plane_exchange(send)
    zall = depth_sum(zbuf)
    zacc, send = middle(units, peer_lists, recv, zall)
    far = plane_exchange(send)
    zsum3 = depth_sum(zacc)
    gr, part = far_products(3, idx, my_z, scalars, r1, w, far, zsum3, hblocks, b, g0, zsum1)

    both = lax.all_gather(jnp.stack([b, r1]), "cols", axis=2, tiled=True)
    gram = pl.pallas_call(
        gram_kernel,
        out_shape=jax.ShapeDtypeStruct((8 * VEC, 4 * VEC), F32),
        compiler_params=PARAMS,
        name="gram",
    )(both, b, r1, g0, gr)
    packed = jnp.concatenate([jnp.pad(gram, ((0, 0), (0, BLK - 4 * VEC))), part], axis=0)
    packed = lax.psum(packed, "rows", axis_index_groups=DEPTH_GROUPS)
    packed = lax.psum(packed, "rows", axis_index_groups=PLANE_GROUPS)

    rr0 = zsum1[DEPTH * ROWS, :, 0]
    d0 = zsum2[DEPTH * ROWS, :, 0] + base_shift * rr0
    rr1 = zsum3[DEPTH * ROWS, :, 0]
    d1 = packed[8 * VEC :, 0]
    alpha0 = rr0 / d0
    beta = rr1 / rr0
    alpha1 = rr1 / d1
    delta = (shifts - base_shift)[:, None]
    zeta1 = 1.0 / (1.0 + delta * alpha0)
    zeta2 = zeta1 * alpha0 / (alpha1 * beta * (1.0 - zeta1) + alpha0 * (1.0 + delta * alpha1))
    weights = filter_weights[:, None]
    coef_b = jnp.sum(weights * (alpha0 * zeta1 + alpha1 * beta * zeta1 * zeta2), axis=0)
    coef_r = jnp.sum(weights * (alpha1 * zeta2), axis=0)
    filtered = coef_b[None, :, None] * b + coef_r[None, :, None] * r1
    all_coef = lax.all_gather(jnp.stack([coef_b, coef_r]), "cols", axis=1, tiled=True)
    left_b, left_r = all_coef[0][:, None], all_coef[1][:, None]
    top, low = packed[: 4 * VEC], packed[4 * VEC : 8 * VEC]
    mixed = left_b * top + left_r * low
    n = VEC
    gram_matrix = mixed[:, :n] * coef_b + mixed[:, n : 2 * n] * coef_r
    ritz = mixed[:, 2 * n : 3 * n] * coef_b + mixed[:, 3 * n : 4 * n] * coef_r
    ritz = ritz + center[0] * gram_matrix
    return filtered, gram_matrix / TOTAL_ROWS, ritz / TOTAL_ROWS


def solution(mesh):
    placed = (P("rows", None, None, None), P("rows", None), P("rows", "cols", None), P(), P(), P())
    return jax.shard_map(
        shards,
        mesh=mesh,
        in_specs=placed,
        out_specs=(P("rows", "cols", None), P(None, "cols"), P(None, "cols")),
        check_vma=False,
    )
```

time: 1120 us -> 719 us (0.64)
  blocking collectives: 638 us -> 20.8 us
  waiting for transfers between devices: 232 us -> 569 us
  matrix products: 137 us -> 0 us
  Pallas kernels: 0 us -> 64.5 us
  starting transfers between devices: 48.9 us -> 26.5 us
  local copies, waits for them, and re-layouts: 34 us -> 12.3 us
    psum x4 -> x0, blocking collectives: 625 us -> none  [the longest x2 250 us: squares(): return lax.psum(column_dot(vector, vector), 'rows')]
    psum x0 -> x8, waiting for transfers between devices: none -> 549 us  [the longest x6 422 us: depth_sum(): return lax.psum(x, 'rows', axis_index_groups=DEPTH_GROUPS)]
    all_gather x5 -> x0, waiting for transfers between devices: 147 us -> none  [apply_h(): whole_vec = lax.all_gather(vector, 'rows', axis=0, tiled=True)]
    dot_general x37 -> x0, matrix products: 137 us -> none  [the longest x5 49.5 us: apply_h(): jnp.einsum('ikab,ikvb->iva', far_blocks, far_vec, precision=exact_mode)]
    all_to_all x6, waiting for transfers between devices: 84.2 us -> 16.7 us  [plane_exchange(): lax.all_to_all(x, 'rows', split_axis=0, concat_axis=0, tiled=True, axis_i...]
    pallas_call x0 -> x10, Pallas kernels: none -> 64.5 us  [the longest x3 30.4 us: local_products(): pl.pallas_call(functools.partial(local_kernel, units), grid_spec=pltpu.Pr...]
    all_to_all x6, starting transfers between devices: 48.4 us -> 26.2 us  [plane_exchange(): lax.all_to_all(x, 'rows', split_axis=0, concat_axis=0, tiled=True, axis_i...]
    gather x10 -> x0, local copies, waits for them, and re-layouts: 17.3 us -> none  [the longest x5 14.2 us: apply_h(): far_vec = whole_vec[far_cols]]
  transfers between devices with their start and end apart: 11 -> 14, of which waited for: 10 -> 9; matrix products, arithmetic and copies ran while one was open for 10% -> 1% of each run, Pallas kernels for 0% -> 0%
where the time goes in v1:
time: 719 us; the launch traced here: 716 us
  waiting for transfers between devices  569 us (79%)
  Pallas kernels  64.5 us (9%)
  starting transfers between devices  26.5 us (4%)
  blocking collectives  20.8 us (3%)
  between operations  14.9 us (2%)
  local copies, waits for them, and re-layouts  12.3 us (2%)
  other arithmetic  7.9 us (1%)
    psum x6, waiting for transfers between devices, depth_sum(): return lax.psum(x, 'rows', axis_index_groups=DEPTH_GROUPS)  422 us
    psum x1, waiting for transfers between devices, shards(): packed = lax.psum(packed, 'rows', axis_index_groups=DEPTH_GROUPS)  67.3 us
    psum x1, waiting for transfers between devices, shards(): packed = lax.psum(packed, 'rows', axis_index_groups=PLANE_GROUPS)  59.6 us
    pallas_call x3, Pallas kernels, local_products(): pl.pallas_call(functools.partial(local_kernel, units), grid_spec=pltpu.Pr...  30.4 us
    pallas_call x3, Pallas kernels, far_products(): pl.pallas_call(functools.partial(far_kernel, stage), grid_spec=pltpu.Pref...  26.3 us
    all_to_all x6, starting transfers between devices, plane_exchange(): lax.all_to_all(x, 'rows', split_axis=0, concat_axis=0, tiled=True, axis_i...  26.2 us
    all_to_all x6, waiting for transfers between devices, plane_exchange(): lax.all_to_all(x, 'rows', split_axis=0, concat_axis=0, tiled=True, axis_i...  16.7 us
  transfers between devices with their start and end apart: 14, of which 9 were waited for; matrix products, arithmetic and copies ran while one was open for 1% of the time, Pallas kernels for 0%

profile of v1, /device:TPU:2, one launch (start us, length us, event | category | flops | bytes accessed | tf_op | source)
XLA Modules:
  0.0 715.9 jit_solution(2026880747532993994)
XLA Ops:
  7.2 0.8 slice.46
  8.3 0.7 slice_subtract_fusion
  9.2 0.8 fusion.8
  10.1 1.0 constant_dynamic-update-slice_fusion
  11.2 0.9 copy-done.2
  12.1 10.2 %local_products.3 = (f32[144,16,128]{2,1,0:T(8,128)}, f32[8,16,128]{2,1,0:T(8,128)S(1)}) custom-call(s32[8,24]{1,0:T(8,128)S(1)} %pad_add_fusion.idx_ref, f32[8,16,128]{2,1,0:T(8,128)S(1)} %copy-done.2, f32[8,24,128,128]{3,2,1,0:T(8,128)} %hb_ref.5, f32[16,128]{1,0:T(8,128)S(1)} %broadcast_in_dim.16.refs_0_, f32[8,16,128]{2,1,0:T(8,128)S(1)} %pad.8.refs_1_), custom_call_target="tpu_custom_call" | custom-call | tf_op jit(solution)/shard_map/local_products/pallas_call | solution.py:141
  22.3 4.5 all-to-all-start
  26.8 0.7 all-reduce.11.cloned.1.call-update
  27.5 16.6 %all-to-all-done.recv_ref = f32[144,16,128]{2,1,0:T(8,128)S(1)} async-done(((f32[144,16,128]{2,1,0:T(8,128)}), f32[144,16,128]{2,1,0:T(8,128)S(1)}, u32[]{:S(2)}, u32[]{:S(2)}) %all-to-all-start) | async-done | bytes 1179680 | tf_op jit(solution)/shard_map/all_to_all | solution.py:260
  44.1 62.4 %all-reduce.11.cloned.1.call-done.zall_ref = f32[64,16,128]{2,1,0:T(8,128)} async-done(((f32[64,16,128]{2,1,0:T(8,128)}), f32[64,16,128]{2,1,0:T(8,128)}) %all-reduce.11.cloned.1.call-update) | async-done | bytes 524304 | tf_op jit(solution)/shard_map/psum | solution.py:265
  106.6 1.0 copy-done.8
  107.6 2.4 middle.3
  110.0 4.4 all-to-all-start.1
  114.5 0.7 all-reduce.13.cloned.1.call-update
  116.4 0.7 pad_maximum_fusion.1.scal_ref
  117.1 73.5 %all-reduce.13.cloned.1.call-done.zsum_ref.tot_ref.refs_1_.refs_2_ = f32[65,16,128]{2,1,0:T(8,128)} async-done(((f32[65,16,128]{2,1,0:T(8,128)}), f32[65,16,128]{2,1,0:T(8,128)}) %all-reduce.13.cloned.1.call-update) | async-done | bytes 532496 | tf_op jit(solution)/shard_map/psum | solution.py:265
  190.7 1.0 copy-done
  191.7 9.0 %far_products.3 = (f32[64,16,128]{2,1,0:T(8,128)}, f32[8,16,128]{2,1,0:T(8,128)S(1)}, f32[16,128]{1,0:T(8,128)S(1)}) custom-call(s32[8,24]{1,0:T(8,128)S(1)} %pad_add_fusion.idx_ref, s32[1]{0:T(128)} %bitcast.3.z_ref, f32[2]{0:T(128)S(1)} %pad_maximum_fusion.1.scal_ref, f32[8,16,128]{2,1,0:T(8,128)S(1)} %copy-done.3, ...), custom_call_target="tpu_custom_call" | custom-call | tf_op jit(solution)/shard_map/far_products/pallas_call | solution.py:196
  200.7 10.1 %local_products.4 = (f32[136,16,128]{2,1,0:T(8,128)}, f32[8,16,128]{2,1,0:T(8,128)S(1)}) custom-call(s32[8,24]{1,0:T(8,128)S(1)} %pad_add_fusion.idx_ref, f32[8,16,128]{2,1,0:T(8,128)S(1)} %get-tuple-element.27.v_ref.refs_1_.g_ref, f32[8,24,128,128]{3,2,1,0:T(8,128)} %hb_ref.5, f32[16,128]{1,0:T(8,128)S(1)} %get-tuple-element.28.refs_0_), custom_call_target="tpu_custom_call" | custom-call | tf_op jit(solution)/shard_map/local_products/pallas_call | solution.py:141
  210.9 4.3 all-to-all-start.2
  215.2 0.7 all-reduce.15.cloned.1.call-update
  215.9 74.8 %all-reduce.15.cloned.1.call-done.zall_ref = f32[64,16,128]{2,1,0:T(8,128)} async-done(((f32[64,16,128]{2,1,0:T(8,128)}), f32[64,16,128]{2,1,0:T(8,128)}) %all-reduce.15.cloned.1.call-update) | async-done | bytes 524304 | tf_op jit(solution)/shard_map/psum | solution.py:265
  290.6 1.0 copy-done.7
  291.7 2.4 middle.4
  294.1 4.4 all-to-all-start.3
  299.1 75.2 %all-reduce.17.cloned.1.call-done.zsum_ref.tot_ref = f32[65,16,128]{2,1,0:T(8,128)} async-done(((f32[65,16,128]{2,1,0:T(8,128)}), f32[65,16,128]{2,1,0:T(8,128)}) %all-reduce.17.cloned.1.call-update) | async-done | bytes 532496 | tf_op jit(solution)/shard_map/psum | solution.py:265
  374.3 1.0 copy-done.4
  375.3 9.1 %far_products.4 = (f32[64,16,128]{2,1,0:T(8,128)}, f32[8,16,128]{2,1,0:T(8,128)S(1)}, f32[16,128]{1,0:T(8,128)S(1)}) custom-call(s32[8,24]{1,0:T(8,128)S(1)} %pad_add_fusion.idx_ref, s32[1]{0:T(128)} %bitcast.3.z_ref, f32[2]{0:T(128)S(1)} %pad_maximum_fusion.1.scal_ref, f32[8,16,128]{2,1,0:T(8,128)S(1)} %get-tuple-element.27.v_ref.refs_1_.g_ref, ...), custom_call_target="tpu_custom_call" | custom-call | tf_op jit(solution)/shard_map/far_products/pallas_call | solution.py:196
  384.4 10.1 %local_products.5 = (f32[136,16,128]{2,1,0:T(8,128)}, f32[8,16,128]{2,1,0:T(8,128)S(1)}) custom-call(s32[8,24]{1,0:T(8,128)S(1)} %pad_add_fusion.idx_ref, f32[8,16,128]{2,1,0:T(8,128)S(1)} %get-tuple-element.34.v_ref.r_ref, f32[8,24,128,128]{3,2,1,0:T(8,128)} %hb_ref.5, f32[16,128]{1,0:T(8,128)S(1)} %get-tuple-element.35.refs_0_), custom_call_target="tpu_custom_call" | custom-call | tf_op jit(solution)/shard_map/local_products/pallas_call | solution.py:141
  394.5 4.3 all-to-all-start.4
  399.4 74.4 %all-reduce.19.cloned.1.call-done.zall_ref = f32[64,16,128]{2,1,0:T(8,128)} async-done(((f32[64,16,128]{2,1,0:T(8,128)}), f32[64,16,128]{2,1,0:T(8,128)}) %all-reduce.19.cloned.1.call-update) | async-done | bytes 524304 | tf_op jit(solution)/shard_map/psum | solution.py:265
  473.8 1.0 copy-done.6
  474.9 2.4 middle.5
  477.3 4.3 all-to-all-start.5
  483.0 13.0 %all_gather.6.all_ref = f32[2,8,64,128]{3,2,1,0:T(8,128)S(1)} all-gather(f32[2,8,16,128]{3,2,1,0:T(8,128)S(1)} %pad_maximum_fusion), channel_id=1, replica_groups=mesh['rows'=64,'cols'=4] {'cols'}, dimensions={2}, use_global_device_ids=true | all-gather | bytes 655360 | tf_op jit(solution)/shard_map/all_gather | solution.py:294
  496.0 61.4 %all-reduce.21.cloned.1.call-done.zsum_ref.tot_ref = f32[65,16,128]{2,1,0:T(8,128)} async-done(((f32[65,16,128]{2,1,0:T(8,128)}), f32[65,16,128]{2,1,0:T(8,128)}) %all-reduce.21.cloned.1.call-update) | async-done | bytes 532496 | tf_op jit(solution)/shard_map/psum | solution.py:265
  557.4 1.0 copy-done.5
  558.5 8.2 %far_products.5 = (f32[8,16,128]{2,1,0:T(8,128)S(1)}, f32[16,128]{1,0:T(8,128)S(1)}) custom-call(s32[8,24]{1,0:T(8,128)S(1)} %pad_add_fusion.idx_ref, s32[1]{0:T(128)} %bitcast.3.z_ref, f32[2]{0:T(128)S(1)} %pad_maximum_fusion.1.scal_ref, f32[8,16,128]{2,1,0:T(8,128)S(1)} %get-tuple-element.34.v_ref.r_ref, f32[8,16,128]{2,1,0:T(8,128)S(1)} %get-tuple-element.39.w_ref, ...), custom_call_target="tpu_custom_call" | custom-call | tf_op jit(solution)/shard_map/far_products/pallas_call | solution.py:196
  568.0 0.8 slice_reduce_fusion.2
  568.8 67.3 %all-reduce.23.cloned.1.call-done = f32[144,128]{1,0:T(8,128)} async-done(((f32[144,128]{1,0:T(8,128)}), f32[144,128]{1,0:T(8,128)}) %all-reduce.23.cloned.1.call-update) | async-done | bytes 73744 | tf_op jit(solution)/shard_map/psum | solution.py:302
  636.1 0.8 slice_reduce_fusion.1
  637.0 59.6 %all-reduce.25.cloned.1.call-done = f32[144,128]{1,0:T(8,128)} async-done(((f32[144,128]{1,0:T(8,128)}), f32[144,128]{1,0:T(8,128)}) %all-reduce.25.cloned.1.call-update) | async-done | bytes 73744 | tf_op jit(solution)/shard_map/psum | solution.py:303
  696.5 0.8 slice_reduce_fusion
  698.1 0.7 multiply_add_fusion
  698.8 7.8 %all-gather = f32[4,16,2]{1,2,0:T(2,128)S(1)} all-gather(f32[1,16,2]{1,2,0:T(2,128)S(1)} %maximum_bitcast_fusion), channel_id=1, replica_groups=mesh['rows'=64,'cols'=4] {'cols'}, dimensions={0}, use_global_device_ids=true | all-gather | bytes 640 | tf_op jit(solution)/shard_map/all_gather | solution.py:319
  706.7 0.9 fusion.4
  707.7 0.7 copy.28
  708.4 0.7 copy.27
  (63 shorter events, 6.3 us)
Async XLA Ops:
  11.1 11.2 %copy-start.9 = (f32[64,16,128]{2,1,0:T(8,128)}, f32[64,16,128]{2,1,0:T(8,128)S(1)}, u32[]{:S(2)}) copy-start(f32[64,16,128]{2,1,0:T(8,128)S(1)} %get-tuple-element.59) | copy-start | bytes 1572868
  11.2 0.9 copy-start.2
  22.3 21.8 %all-to-all-start = ((f32[144,16,128]{2,1,0:T(8,128)}), f32[144,16,128]{2,1,0:T(8,128)S(1)}, u32[]{:S(2)}, u32[]{:S(2)}) async-start(f32[144,16,128]{2,1,0:T(8,128)} %get-tuple-element.23), calls=%async_computation | async-start | bytes 2359296 | tf_op jit(solution)/shard_map/all_to_all | solution.py:260
  26.8 79.8 %all-reduce.11.cloned.1.call-start = ((), (), s32[]{:S(2)}) async-start(), calls=%async_computation.6 | async-start | bytes 1048576 | tf_op jit(solution)/shard_map/psum | solution.py:265
  106.6 1.0 copy-start.8
  110.0 5.8 copy-start.11
  110.0 80.7 %copy-start.3 = (f32[8,16,128]{2,1,0:T(8,128)S(1)}, f32[8,16,128]{2,1,0:T(8,128)}, u32[]{:S(2)}) copy-start(f32[8,16,128]{2,1,0:T(8,128)} %b_ref.1) | copy-start | bytes 196612
  110.0 80.7 %all-to-all-start.1 = ((f32[128,16,128]{2,1,0:T(8,128)}), f32[128,16,128]{2,1,0:T(8,128)S(1)}, u32[]{:S(2)}, u32[]{:S(2)}) async-start(f32[128,16,128]{2,1,0:T(8,128)} %get-tuple-element.26), calls=%async_computation.1 | async-start | bytes 2097152 | tf_op jit(solution)/shard_map/all_to_all | solution.py:260
  114.4 76.2 %all-reduce.13.cloned.1.call-start = ((), (), s32[]{:S(2)}) async-start(), calls=%async_computation.7 | async-start | bytes 1064960 | tf_op jit(solution)/shard_map/psum | solution.py:265
  190.7 1.0 copy-start
  210.9 79.8 %all-to-all-start.2 = ((f32[136,16,128]{2,1,0:T(8,128)}), f32[136,16,128]{2,1,0:T(8,128)S(1)}, u32[]{:S(2)}, u32[]{:S(2)}) async-start(f32[136,16,128]{2,1,0:T(8,128)} %get-tuple-element.29), calls=%async_computation.2 | async-start | bytes 2228224 | tf_op jit(solution)/shard_map/all_to_all | solution.py:260
  215.1 75.5 %all-reduce.15.cloned.1.call-start = ((), (), s32[]{:S(2)}) async-start(), calls=%async_computation.8 | async-start | bytes 1048576 | tf_op jit(solution)/shard_map/psum | solution.py:265
  290.6 1.0 copy-start.7
  294.1 80.2 %copy-start.1 = (f32[65,16,128]{2,1,0:T(8,128)S(1)}, f32[65,16,128]{2,1,0:T(8,128)}, u32[]{:S(2)}) copy-start(f32[65,16,128]{2,1,0:T(8,128)} %all-reduce.13.cloned.1.call-done.zsum_ref.tot_ref.refs_1_.refs_2_) | copy-start | bytes 1597444
  294.1 80.2 %all-to-all-start.3 = ((f32[128,16,128]{2,1,0:T(8,128)}), f32[128,16,128]{2,1,0:T(8,128)S(1)}, u32[]{:S(2)}, u32[]{:S(2)}) async-start(f32[128,16,128]{2,1,0:T(8,128)} %get-tuple-element.33), calls=%async_computation.3 | async-start | bytes 2097152 | tf_op jit(solution)/shard_map/all_to_all | solution.py:260
  298.5 75.7 %all-reduce.17.cloned.1.call-start = ((), (), s32[]{:S(2)}) async-start(), calls=%async_computation.9 | async-start | bytes 1064960 | tf_op jit(solution)/shard_map/psum | solution.py:265
  374.3 1.0 copy-start.4
  394.5 79.3 %all-to-all-start.4 = ((f32[136,16,128]{2,1,0:T(8,128)}), f32[136,16,128]{2,1,0:T(8,128)S(1)}, u32[]{:S(2)}, u32[]{:S(2)}) async-start(f32[136,16,128]{2,1,0:T(8,128)} %get-tuple-element.36), calls=%async_computation.4 | async-start | bytes 2228224 | tf_op jit(solution)/shard_map/all_to_all | solution.py:260
  398.8 75.0 %all-reduce.19.cloned.1.call-start = ((), (), s32[]{:S(2)}) async-start(), calls=%async_computation.10 | async-start | bytes 1048576 | tf_op jit(solution)/shard_map/psum | solution.py:265
  473.8 1.0 copy-start.6
  477.3 80.2 %all-to-all-start.5 = ((f32[128,16,128]{2,1,0:T(8,128)}), f32[128,16,128]{2,1,0:T(8,128)S(1)}, u32[]{:S(2)}, u32[]{:S(2)}) async-start(f32[128,16,128]{2,1,0:T(8,128)} %get-tuple-element.40), calls=%async_computation.5 | async-start | bytes 2097152 | tf_op jit(solution)/shard_map/all_to_all | solution.py:260
  481.6 75.9 %all-reduce.21.cloned.1.call-start = ((), (), s32[]{:S(2)}) async-start(), calls=%async_computation.11 | async-start | bytes 1064960 | tf_op jit(solution)/shard_map/psum | solution.py:265
  482.1 154.0 %all-reduce.23.cloned.1.call-start = ((), (), s32[]{:S(2)}) async-start(), calls=%async_computation.12 | async-start | bytes 147456 | tf_op jit(solution)/shard_map/psum | solution.py:302
  557.4 1.0 copy-start.5
  566.7 131.3 %copy-start.10 = (f32[8]{0:T(128)S(1)}, f32[8]{0:T(128)}, u32[]{:S(2)}) copy-start(f32[8]{0:T(128)} %param.11) | copy-start | bytes 100
  568.0 128.6 %all-reduce.25.cloned.1.call-start = ((), (), s32[]{:S(2)}) async-start(), calls=%async_computation.13 | async-start | bytes 147456 | tf_op jit(solution)/shard_map/psum | solution.py:303
Sparse Core Ops, SparseCore 0:
  29.9 76.6 all-reduce.10
  117.7 72.8 all-reduce.12
  218.4 72.1 all-reduce.14
  301.4 72.8 all-reduce.16
  401.6 72.1 all-reduce.18
  484.6 72.8 all-reduce.20
  568.1 67.9 all-reduce.22
  638.4 58.0 all-reduce.24
